TPU v7x, 32 devices: a whole 2x2x4 slice. The times are simulated.
32 devices in a mesh: req: 4 (over y, x), seq: 8 (over z, core).
Axes of the slice: x: 2, y: 2, z: 4, core: 2. Of those that a mesh axis runs over, the one named last changes fastest.
Arguments:
- sequence_sizes: int32 [4], P('req'), may hold values from 128 to 2048, as said below
- acceptor: bfloat16 [4, 2048, 2048], P('req', 'seq'), may hold values from -6 to 6
- fading_scores: bfloat16 [4, 2048, 2048], P('req', 'seq'), may hold values from -20 to 6
- address_source: bfloat16 [4, 2048, 2048], P('req', 'seq'), may hold values from -6 to 6
- payload_source: bfloat16 [4, 2048, 2048], P('req', 'seq'), may hold values from -40 to 40
- learning_speed_scores: bfloat16 [4, 2048, 2048], P('req', 'seq'), may hold values from -20 to 6
- exit_switch: bfloat16 [4, 2048, 2048], P('req', 'seq'), may hold values from -6 to 6
- address_removal_factor: float32 [2048], replicated, may hold values from 0.4 to 1.6
- address_learning_factor: float32 [2048], replicated, may hold values from 0.3 to 1.5
- present_extra_factor: float32 [2048], replicated, may hold values from -0.9 to 0.9
- cluster_scale_term: float32 [2048], replicated, may hold values from 0.1 to 1.9
- cluster_shift_term: float32 [2048], replicated, may hold values from -1.8 to 1.8
- final_projection: bfloat16 [2048, 4096], P(('req', 'seq')), may hold values from -0.125 to 0.125
Outputs:
- mixed_out: bfloat16 [4, 2048, 4096], P('req', 'seq')
Inputs may be any that keep to these rules, and one draw needn't show every extreme that they name: `sequence_sizes`: each length is a multiple of 128, and in every draw some request has all 2048 tokens.
All inputs are finite; a program needn't handle non-finite values.
Results may differ from a plain program's by a relative error of at most 0.0049.
Values may be sent and summed in bfloat16 or wider, within the bound.
A program may use at most 256 MiB of HBM per device.

v0:
```python
import math

import jax
import jax.numpy as jnp
from jax import lax
from jax.sharding import PartitionSpec as P

LOCAL_UNITS = 32


DECAY_SCALE = 0.606531
UNIT_EPS = 1e-06
GROUP_EPS = 0.00064
EXACT = lax.Precision.HIGHEST
BLOCK_LIMIT = 64


def prefix(array, axis, combine, identity):
    count, position = (lax.axis_size(axis), lax.axis_index(axis))
    everything = jax.tree.map(lambda part: lax.all_gather(part, axis), array)
    start = jax.tree.map(
        lambda part, zero: jnp.broadcast_to(jnp.asarray(zero, part.dtype), part.shape),
        array,
        identity,
    )

    def hop(k, before):
        reached = k < position
        new = combine(before, jax.tree.map(lambda part: part[k], everything))
        return jax.tree.map(lambda a, b: jnp.where(reached, a, b), new, before)

    return lax.fori_loop(0, count, hop, start)


def prepare(
    acceptor,
    fading_scores,
    address_source,
    payload_source,
    learning_speed_scores,
    address_removal_factor,
    address_learning_factor,
    live_entries,
):
    head_shape = (acceptor.shape[0], LOCAL_UNITS, acceptor.shape[1] // LOCAL_UNITS)
    learn_rate = jax.nn.sigmoid(learning_speed_scores.astype(jnp.float32))
    key_vals = address_source.astype(jnp.float32)
    unit_dir = (key_vals * address_removal_factor).reshape(head_shape)
    unit_dir = unit_dir * lax.rsqrt(jnp.sum(unit_dir * unit_dir, -1, keepdims=True) + UNIT_EPS)
    address_scaled = (
        key_vals * (1.0 + (learn_rate - 1.0) * address_learning_factor) * live_entries
    ).reshape(head_shape)
    log_decay = (
        -DECAY_SCALE * jax.nn.sigmoid(fading_scores.astype(jnp.float32)) * live_entries
    ).reshape(head_shape)
    payload_lines = (payload_source.astype(jnp.float32) * live_entries).reshape(head_shape)
    removal = (learn_rate * live_entries).reshape(head_shape)
    acceptor_real = acceptor.astype(jnp.float32).reshape(head_shape)
    return (acceptor_real, log_decay, address_scaled, payload_lines, -unit_dir, unit_dir * removal)


def masked_pairs(left_side, right_side, keep_mask):
    paired = jnp.einsum("thk,shk->hts", left_side, right_side, precision=EXACT)
    return jnp.where(keep_mask, paired, 0.0)


def block_pass(carried, pieces):
    acceptor_real, log_decay, address_scaled, payload_lines, pull_dir, push_dir = pieces
    block_len = acceptor_real.shape[0]
    cumul = jnp.cumsum(log_decay, 0)
    growth = jnp.exp(-cumul)
    pull_now = pull_dir * jnp.exp(cumul - log_decay)
    read_now = acceptor_real * jnp.exp(cumul)
    push_back = push_dir * growth
    key_back = address_scaled * growth
    places = jnp.arange(block_len)
    strict = (places[:, None] > places[None, :])[None]
    inclusive = (places[:, None] >= places[None, :])[None]
    pull_push = masked_pairs(pull_now, push_back, strict)
    pull_key = masked_pairs(pull_now, key_back, strict)
    read_push = masked_pairs(read_now, push_back, inclusive)
    read_key = masked_pairs(read_now, key_back, inclusive)
    source = jnp.einsum("thk,hrk->htr", pull_now, carried, precision=EXACT) + jnp.einsum(
        "hts,shr->htr", pull_key, payload_lines, precision=EXACT
    )
    system = jnp.eye(block_len, dtype=jnp.float32)[None] - pull_push
    removed = jax.scipy.linalg.solve_triangular(system, source, lower=True, unit_diagonal=True)
    result = (
        jnp.einsum("thk,hrk->htr", read_now, carried, precision=EXACT)
        + jnp.einsum("hts,hsr->htr", read_push, removed, precision=EXACT)
        + jnp.einsum("hts,shr->htr", read_key, payload_lines, precision=EXACT)
    )
    tail_decay = jnp.exp(cumul[-1:] - cumul)
    carried = (
        carried * jnp.exp(cumul[-1])[:, None, :]
        + jnp.einsum("hsr,shk->hrk", removed, push_dir * tail_decay, precision=EXACT)
        + jnp.einsum("shr,shk->hrk", payload_lines, address_scaled * tail_decay, precision=EXACT)
    )
    return (carried, result)


def run_local(carried, pieces, block_len):
    element_sum = pieces[0].shape[0]
    block_count = element_sum // block_len
    stacked = tuple((piece.reshape((block_count, block_len) + piece.shape[1:]) for piece in pieces))
    carried, results = lax.scan(block_pass, carried, stacked)
    row_count = results.shape[-1]
    results = jnp.transpose(results, (0, 2, 1, 3)).reshape(element_sum, LOCAL_UNITS, row_count)
    return (results, carried)


def compose_maps(earlier, later):
    transit = jnp.einsum("hij,hjk->hik", earlier[0], later[0], precision=EXACT)
    offset = jnp.einsum("hvj,hjk->hvk", earlier[1], later[0], precision=EXACT) + later[1]
    return (transit, offset)


def per_device(
    sequence_sizes,
    acceptor,
    fading_scores,
    address_source,
    payload_source,
    learning_speed_scores,
    exit_switch,
    address_removal_factor,
    address_learning_factor,
    present_extra_factor,
    cluster_scale_term,
    cluster_shift_term,
    final_projection,
):
    element_sum = acceptor.shape[1]
    feature_sum = acceptor.shape[2]
    unit_features = feature_sum // LOCAL_UNITS
    seq_index = lax.axis_index("seq")
    position = seq_index * element_sum + jnp.arange(element_sum, dtype=jnp.int32)
    live_entries = (position < sequence_sizes[0]).astype(jnp.float32)[:, None]
    acceptor_real, log_decay, address_scaled, payload_lines, pull_dir, push_dir = prepare(
        acceptor[0],
        fading_scores[0],
        address_source[0],
        payload_source[0],
        learning_speed_scores[0],
        address_removal_factor,
        address_learning_factor,
        live_entries,
    )
    block_len = math.gcd(BLOCK_LIMIT, element_sum)
    square_eye = jnp.broadcast_to(
        jnp.eye(unit_features, dtype=jnp.float32), (LOCAL_UNITS, unit_features, unit_features)
    )
    blank_state = jnp.zeros((LOCAL_UNITS, unit_features, unit_features), jnp.float32)
    initial = jnp.concatenate([blank_state, square_eye], 1)
    extended = jnp.concatenate([payload_lines, jnp.zeros_like(payload_lines)], 2)
    results, final_state = run_local(
        initial, (acceptor_real, log_decay, address_scaled, extended, pull_dir, push_dir), block_len
    )
    before = prefix(
        (final_state[:, unit_features:], final_state[:, :unit_features]),
        "seq",
        compose_maps,
        (square_eye, blank_state),
    )
    wkv_out = results[..., :unit_features] + jnp.einsum(
        "hvk,thk->thv", before[1], results[..., unit_features:], precision=EXACT
    )
    center = wkv_out - jnp.mean(wkv_out, -1, keepdims=True)
    standardized_lines = center * lax.rsqrt(
        jnp.mean(center * center, -1, keepdims=True) + GROUP_EPS
    )
    standardized_lines = (
        standardized_lines.reshape(element_sum, feature_sum) * cluster_scale_term
        + cluster_shift_term
    )
    extra_share = (
        jnp.sum(
            acceptor_real
            * address_scaled
            * present_extra_factor.reshape(LOCAL_UNITS, unit_features),
            -1,
            keepdims=True,
        )
        * payload_lines
    )
    blended_entry = (
        (standardized_lines + extra_share.reshape(element_sum, feature_sum))
        * exit_switch[0].astype(jnp.float32)
        * live_entries
    ).astype(jnp.bfloat16)
    projected = jnp.dot(
        blended_entry,
        lax.all_gather(final_projection, ("req", "seq"), axis=0, tiled=True),
        preferred_element_type=jnp.float32,
    )
    return projected.astype(jnp.bfloat16)[None]


def solution(mesh):
    placed = (
        P("req"),
        P("req", "seq", None),
        P("req", "seq", None),
        P("req", "seq", None),
        P("req", "seq", None),
        P("req", "seq", None),
        P("req", "seq", None),
        P(),
        P(),
        P(),
        P(),
        P(),
        P(("req", "seq"), None),
    )
    return jax.shard_map(
        per_device, mesh=mesh, in_specs=placed, out_specs=P("req", "seq", None), check_vma=False
    )
```

profile of v0, /device:TPU:0, one launch (start us, length us, event | category | flops | bytes accessed | tf_op | source)
XLA Modules:
  0.0 1042.8 jit_solution(6081047184247445910)
XLA Ops:
  30.7 5.3 copy.82
  36.0 5.4 copy.79
  51.1 5.4 copy.77
  67.9 5.5 multiply_multiply_fusion
  73.3 665.0 %while.26 = (s32[]{:T(128)}, f32[32,128,64]{1,2,0:T(8,128)S(1)}, f32[4,32,64,128]{3,1,2,0:T(8,128)}, f32[4,64,32,64]{3,2,1,0:T(8,128)}, f32[4,64,32,64]{3,2,1,0:...) while((s32[]{:T(128)}, f32[32,128,64]{1,2,0:T(8,128)S(1)}, ...), condition=%wide.region_3.4_spmd, body=%wide.region_1.3_spmd.sunk | while | flops 2025222144 | bytes 80357200 | solution.py:106
  81.2 5.3 bitcast_multiply_fusion.9
  127.8 7.5 broadcast_select_fusion.6
  144.4 68.6 %custom-call.7 = f32[32,1,64,64]{0,2,3,1:T(8,128)} custom-call(f32[32,1,64,64]{0,3,2,1:T(8,128)} %get-tuple-element.351), custom_call_target="InvertDiagBlocksLowerTriangular" | custom-call | tf_op jit(solution)/shard_map/while/body/eval_jaxpr/jit(_solve_triangular)/vmap()/triangular_solve | solution.py:87
  245.1 5.3 bitcast_multiply_fusion.9
  291.4 7.5 broadcast_select_fusion.6
  308.0 68.8 %custom-call.7 = f32[32,1,64,64]{0,2,3,1:T(8,128)} custom-call(f32[32,1,64,64]{0,3,2,1:T(8,128)} %get-tuple-element.351), custom_call_target="InvertDiagBlocksLowerTriangular" | custom-call | tf_op jit(solution)/shard_map/while/body/eval_jaxpr/jit(_solve_triangular)/vmap()/triangular_solve | solution.py:87
  408.7 5.3 bitcast_multiply_fusion.9
  455.3 7.5 broadcast_select_fusion.6
  471.9 68.6 %custom-call.7 = f32[32,1,64,64]{0,2,3,1:T(8,128)} custom-call(f32[32,1,64,64]{0,3,2,1:T(8,128)} %get-tuple-element.351), custom_call_target="InvertDiagBlocksLowerTriangular" | custom-call | tf_op jit(solution)/shard_map/while/body/eval_jaxpr/jit(_solve_triangular)/vmap()/triangular_solve | solution.py:87
  572.6 5.3 bitcast_multiply_fusion.9
  618.9 7.5 broadcast_select_fusion.6
  635.5 68.8 %custom-call.7 = f32[32,1,64,64]{0,2,3,1:T(8,128)} custom-call(f32[32,1,64,64]{0,3,2,1:T(8,128)} %get-tuple-element.351), custom_call_target="InvertDiagBlocksLowerTriangular" | custom-call | tf_op jit(solution)/shard_map/while/body/eval_jaxpr/jit(_solve_triangular)/vmap()/triangular_solve | solution.py:87
  741.9 8.1 fusion.52
  759.0 66.4 %all-gather.8.cloned.1.call-done = f32[256,64,64]{2,1,0:T(8,128)} async-done(((f32[32,64,64]{2,1,0:T(8,128)}), f32[256,64,64]{2,1,0:T(8,128)}) %all-gather.8.cloned.1.call-update) | async-done | bytes 4194320 | tf_op jit(solution)/shard_map/all_gather | solution.py:20
  825.4 82.2 %all-gather.10.cloned.1.call-done = f32[256,64,64]{2,1,0:T(8,128)} async-done(((f32[32,64,64]{2,1,0:T(8,128)}), f32[256,64,64]{2,1,0:T(8,128)}) %all-gather.10.cloned.1.call-update) | async-done | bytes 4194320 | tf_op jit(solution)/shard_map/all_gather | solution.py:20
  907.6 39.0 %while.27 = (s32[]{:T(128)}, f32[32,64,64]{1,2,0:T(8,128)S(1)}, s32[]{:T(128)}, f32[8,32,64,64]{3,2,1,0:T(8,128)}, f32[8,32,64,64]{3,2,1,0:T(8,128)}, /*index=5*/s32[]{:T(128)}, s32[]{:T(128)}) while((s32[]{:T(128)}, f32[32,64,64]{1,2,0:T(8,128)S(1)}, s32[]{:T(128)}, f32[8,32,64,64]{3,2,1,0:T(8,128)}, f32[8,32,64,64]{3,2,1,0:T(8,128)}, ...), condition=%wide.region_5.6_spmd.clone, body=%wide.region_4.5_spmd.clone.sunk | while | flops 101187584 | bytes 7866467 | solution.py:32
  946.6 10.2 fusion.54
  960.6 63.5 %all-gather.6.cloned.1.call-done = bf16[2048,4096]{1,0:T(8,128)(2,1)} async-done(((bf16[64,4096]{1,0:T(8,128)(2,1)}), bf16[2048,4096]{1,0:T(8,128)(2,1)}) %all-gather.6.cloned.1.call-update) | async-done | bytes 16777232 | tf_op jit(solution)/shard_map/all_gather | solution.py:193
  1024.1 11.7 %fusion.37 = bf16[1,256,4096]{2,1,0:T(8,128)(2,1)} fusion(bf16[256,2048]{0,1:T(8,128)(2,1)S(1)} %fusion.42, bf16[2048,4096]{1,0:T(8,128)(2,1)} %all-gather.6.cloned.1.call-done), kind=kOutput, calls=%fused_computation.69 | convolution fusion | flops 4296015872 | bytes 19922944 | tf_op jit(solution)/shard_map/dot_general | solution.py:191
  (304 shorter events, 426.3 us)
Async XLA Ops:
  6.5 818.8 %all-gather.8.cloned.1.call-start = ((), (), s32[]{:S(2)}) async-start(), calls=%async_computation.1 | async-start | bytes 9437184 | tf_op jit(solution)/shard_map/all_gather | solution.py:20
  9.5 3.2 copy-start.16
  14.7 3.8 copy-start.17
  22.5 4.9 copy-start.10
  22.7 4.8 copy-start.18
  36.0 5.5 copy-start.12
  61.6 4.8 copy-start.8
  61.6 6.2 copy-start.9
  138.6 3.1 copy-start.7
  219.6 4.0 copy-start.1
  231.5 2.5 copy-start.4
  302.2 3.1 copy-start.7
  383.5 4.0 copy-start.1
  395.4 2.5 copy-start.4
  466.1 3.1 copy-start.7
  547.1 4.0 copy-start.1
  559.0 2.5 copy-start.4
  629.7 3.1 copy-start.7
  711.0 4.0 copy-start.1
  722.9 2.5 copy-start.4
  740.4 167.1 %all-gather.10.cloned.1.call-start = ((), (), s32[]{:S(2)}) async-start(), calls=%async_computation.2 | async-start | bytes 9437184 | tf_op jit(solution)/shard_map/all_gather | solution.py:20
  741.2 282.9 %all-gather.6.cloned.1.call-start = ((), (), s32[]{:S(2)}) async-start(), calls=%async_computation | async-start | bytes 17301504 | tf_op jit(solution)/shard_map/all_gather | solution.py:193
  750.0 4.8 copy-start.22
  754.9 2.5 copy-start.13
  (28 other events, 48.7 us)
Sparse Core Ops, SparseCore 0:
  740.6 84.7 all-gather.7
  827.0 80.5 all-gather.9
  910.6 113.4 all-gather.5
where the time goes:
time: 1060 us; the launch traced here: 1040 us
  other arithmetic  373 us (35%)
  local copies, waits for them, and re-layouts  226 us (21%)
  waiting for transfers between devices  213 us (20%)
  matrix products  203 us (19%)
  between operations  14.5 us (1%)
  loops' own time  12.3 us (1%)
    another operation x8, other arithmetic, block_pass(): jax.scipy.linalg.solve_triangular(system, source, lower=True, unit_diagon...  275 us
    all_gather x2, waiting for transfers between devices, prefix(): everything = jax.tree.map(lambda part: lax.all_gather(part, axis), array)  149 us
    dot_general x16, matrix products, masked_pairs(): paired = jnp.einsum('thk,shk->hts', left_side, right_side, precision=EXACT)  77.7 us
    all_gather x1, waiting for transfers between devices, per_device(): lax.all_gather(final_projection, ('req', 'seq'), axis=0, tiled=True)  63.5 us
    dot_general x16, local copies, waits for them, and re-layouts, masked_pairs(): paired = jnp.einsum('thk,shk->hts', left_side, right_side, precision=EXACT)  51.5 us
    select_n x8, other arithmetic, masked_pairs(): return jnp.where(keep_mask, paired, 0.0)  47.3 us
    select_n x12, local copies, waits for them, and re-layouts, masked_pairs(): return jnp.where(keep_mask, paired, 0.0)  36.8 us
    dynamic_slice x12, local copies, waits for them, and re-layouts, run_local(): carried, results = lax.scan(block_pass, carried, stacked)  26.3 us
  transfers between devices with their start and end apart: 3, of which 3 were waited for; matrix products, arithmetic and copies ran while one was open for 7% of the time, Pallas kernels for 0%

commit v1 on v0

v1 whole, which is shorter than its diff:
```python
import functools
import math

import jax
import jax.numpy as jnp
import numpy as np
from jax import lax
from jax.experimental import pallas as pl
from jax.experimental.pallas import tpu as pltpu
from jax.sharding import PartitionSpec as P

LOCAL_UNITS = 32
DECAY_SCALE = 0.606531
UNIT_EPS = 1e-06
GROUP_EPS = 0.00064
F32, BF16 = jnp.float32, jnp.bfloat16
UNIT = 64
PAIR = 128


def split2(x):
    hi = x.astype(BF16)
    return hi, (x - hi.astype(F32)).astype(BF16)


def mm(a, b):
    return jnp.dot(a, b, preferred_element_type=F32)


def mm_t(a, b):
    return lax.dot_general(a, b, (((1,), (1,)), ((), ())), preferred_element_type=F32)


def square_product(a, b):
    (ah, al), (bh, bl) = a, b
    left = jnp.concatenate([ah, al], 1)
    row = jnp.concatenate([bh, bl], 1)
    both = mm(left, jnp.concatenate([row, row], 0))
    return both[:, :PAIR] + both[:, PAIR:]


def wide_product(a, b):
    (ah, al), (bh, bl) = a, b
    both = mm(ah, jnp.concatenate([bh, bl], 1))
    return both[:, :PAIR] + both[:, PAIR:] + mm(al, bh)


def head_sum(x, ones):
    hi, lo = split2(x)
    return mm(hi, ones) + mm(lo, ones)


def sigmoid(x):
    return 1.0 / (1.0 + jnp.exp(-x))


def local_kernel(
    live_ref, acc_ref, fade_ref, key_ref, val_ref, rate_ref, rem_ref, learn_ref, extra_ref,
    tri_ref, ones_ref, level_ref, out_ref, query_ref, bonus_ref, state_ref,
):
    tokens = acc_ref.shape[0]
    half = tokens // 2
    ones = ones_ref[...]
    live = live_ref[...]
    rate = sigmoid(rate_ref[...].astype(F32))
    keys = key_ref[...].astype(F32)
    unit = keys * rem_ref[...]
    unit = unit * lax.rsqrt(head_sum(unit * unit, ones) + UNIT_EPS)
    key_mod = keys * (1.0 + (rate - 1.0) * learn_ref[...]) * live
    log_decay = -DECAY_SCALE * sigmoid(fade_ref[...].astype(F32)) * live
    values = val_ref[...] * live.astype(BF16)
    acc = acc_ref[...].astype(F32)
    bonus_ref[...] = head_sum(acc * key_mod * extra_ref[...], ones) * values.astype(F32)
    push = unit * (rate * live)

    first, rest = split2(log_decay)
    third = (log_decay - first.astype(F32) - rest.astype(F32)).astype(BF16)
    tri = tri_ref[...]
    cumul = mm(tri, first) + (mm(tri, rest) + mm(tri, third))
    middle = cumul[half - 1 : half]
    last = cumul[tokens - 1 : tokens]
    up = jnp.exp(cumul - middle)
    down = jnp.exp(middle - cumul)
    to_middle = jnp.exp(middle)
    tail = jnp.exp(last - cumul)
    read_c = acc * up
    pull_c = -unit * jnp.exp(cumul - log_decay - middle)
    push_c = split2(push * down)
    key_c = split2(key_mod * down)
    read_true = read_c * to_middle
    pull_true = pull_c * to_middle
    push_tail = (push * tail).T
    key_tail = (key_mod * tail).T
    whole_decay = jnp.exp(last)

    lane = lax.broadcasted_iota(jnp.int32, (1, PAIR), 1)
    rows = lax.broadcasted_iota(jnp.int32, (tokens, tokens), 0)
    columns = lax.broadcasted_iota(jnp.int32, (tokens, tokens), 1)
    right = jnp.concatenate([push_c[0], key_c[0]], 0)
    right_low = jnp.concatenate([push_c[1], key_c[1]], 0)
    right_twice = jnp.concatenate([right, right], 1)
    pulled_swap = pltpu.roll(pull_true, UNIT, 1)
    read_swap = pltpu.roll(read_true, UNIT, 1)
    eye = (rows[:half, :half] == columns[:half, :half]).astype(F32)
    krow = lax.broadcasted_iota(jnp.int32, (UNIT, PAIR), 0)
    klane = lax.broadcasted_iota(jnp.int32, (UNIT, PAIR), 1)
    decay_swap = pltpu.roll(whole_decay * jnp.ones((8, PAIR), F32), UNIT, 1)[:1]
    levels = level_ref.shape[0]
    outs = []
    for h in range(2):
        mine = (lane // UNIT) == h
        ph, plow = split2(jnp.where(mine, pull_c, 0.0))
        rh, rlow = split2(jnp.where(mine, read_c, 0.0))
        left = jnp.concatenate(
            [jnp.concatenate([ph, plow], 1), jnp.concatenate([rh, rlow], 1)], 0
        )
        pairs = mm_t(left, right_twice) + mm_t(jnp.concatenate([ph, rh], 0), right_low)
        a_pp = jnp.where(rows > columns, pairs[:tokens, :tokens], 0.0)
        a_pk = split2(jnp.where(rows > columns, pairs[:tokens, tokens:], 0.0))
        a_rp = split2(jnp.where(rows >= columns, pairs[tokens:, :tokens], 0.0))
        a_rk = split2(jnp.where(rows >= columns, pairs[tokens:, tokens:], 0.0))
        system_h, system_l = split2(a_pp)
        inverses = []
        for b in range(2):
            cut = slice(b * half, (b + 1) * half)
            block_h, block_l = system_h[cut, cut], system_l[cut, cut]
            inverse = eye + a_pp[cut, cut] * level_ref[0].astype(F32)
            for level in range(1, levels):
                mask = level_ref[level]
                now = split2(inverse)
                step = square_product((block_h * mask, block_l * mask), now)
                inverse = inverse + square_product(now, split2(step))
            inverses.append(split2(inverse))
        source = jnp.where(mine, mm(a_pk[0], values) + mm(a_pk[1], values), pulled_swap)
        top = square_product(inverses[0], split2(source[:half]))
        top_s = split2(top)
        below = source[half:] + square_product(
            (system_h[half:, :half], system_l[half:, :half]), top_s
        )
        bottom = square_product(inverses[1], split2(below))
        bottom_s = split2(bottom)
        removed = (
            jnp.concatenate([top_s[0], bottom_s[0]], 0),
            jnp.concatenate([top_s[1], bottom_s[1]], 0),
        )
        result = wide_product(a_rp, removed) + jnp.where(
            mine, mm(a_rk[0], values) + mm(a_rk[1], values), read_swap
        )
        outs.append(result)
        own = slice(h * UNIT, (h + 1) * UNIT)
        kt = split2(key_tail[own])
        identity = jnp.where(klane == krow + (1 - h) * UNIT, decay_swap, 0.0)
        state = wide_product(split2(push_tail[own]), removed) + jnp.where(
            mine, mm(kt[0], values) + mm(kt[1], values), identity
        )
        state_ref[h] = state if h == 0 else pltpu.roll(state, UNIT, 1)
    low = lane < UNIT
    out_ref[...] = jnp.where(low, outs[0], outs[1])
    query_ref[...] = pltpu.roll(jnp.where(low, outs[1], outs[0]), UNIT, 1)


def local_pass(live, acceptor, fading, keys, values, rates, removal, learning, extra):
    tokens, width = acceptor.shape
    half = tokens // 2
    tri = jnp.asarray(np.tril(np.ones((tokens, tokens), np.float32)), BF16)
    places = np.arange(PAIR)
    ones = jnp.asarray(places[:, None] // UNIT == places[None, :] // UNIT, BF16)
    spots = np.arange(half)
    apart = spots[:, None] ^ spots[None, :]
    levels = jnp.asarray(
        np.stack([(apart >> n) == 1 for n in range(int(math.log2(half)))]), BF16
    )
    token_block = pl.BlockSpec((tokens, PAIR), lambda i: (0, i))
    row_block = pl.BlockSpec((1, PAIR), lambda i: (0, i))

    def fixed(shape):
        return pl.BlockSpec(shape, lambda i: (0,) * len(shape))

    return pl.pallas_call(
        local_kernel,
        grid=(width // PAIR,),
        in_specs=[fixed((tokens, 1))]
        + [token_block] * 5
        + [row_block] * 3
        + [fixed(tri.shape), fixed(ones.shape), fixed(levels.shape)],
        out_specs=[token_block] * 3 + [pl.BlockSpec((2, UNIT, PAIR), lambda i: (i, 0, 0))],
        out_shape=[jax.ShapeDtypeStruct((tokens, width), F32)] * 3
        + [jax.ShapeDtypeStruct((width // UNIT, UNIT, PAIR), F32)],
        compiler_params=pltpu.CompilerParams(vmem_limit_bytes=40 * 1024 * 1024),
        cost_estimate=pl.CostEstimate(
            flops=60 * 10**9, bytes_accessed=12 * 2**20, transcendentals=3 * 10**6
        ),
    )(live, acceptor, fading, keys, values, rates, removal, learning, extra, tri, ones, levels)


def prefix_kernel(blocks, heads, map_ref, before_ref):
    lane = lax.broadcasted_iota(jnp.int32, (1, PAIR), 1)
    low = lane < UNIT
    for h in range(heads):
        before_ref[h] = jnp.zeros((UNIT, PAIR), F32)
    states = [jnp.where(low, map_ref[h], 0.0) for h in range(heads)]
    for n in range(1, blocks):
        for h in range(heads):
            before_ref[n * heads + h] = states[h]
            if n + 1 < blocks:
                step = map_ref[n * heads + h]
                transit = pltpu.roll(step, UNIT, 1)[:, :UNIT]
                states[h] = jnp.where(low, step, 0.0) + jnp.dot(
                    transit, states[h], precision=lax.Precision.HIGHEST,
                    preferred_element_type=F32,
                )


def state_before(maps, axis):
    blocks = lax.axis_size(axis)
    heads = maps.shape[0] // blocks
    mine = lax.all_to_all(maps, axis, 0, 0, tiled=True)
    before = pl.pallas_call(
        functools.partial(prefix_kernel, blocks, heads),
        out_shape=jax.ShapeDtypeStruct(mine.shape, F32),
        compiler_params=pltpu.CompilerParams(vmem_limit_bytes=24 * 1024 * 1024),
    )(mine)
    return lax.all_to_all(before, axis, 0, 0, tiled=True)


def finish_kernel(
    live_ref, out_ref, query_ref, bonus_ref, before_ref, switch_ref, gain_ref, shift_ref,
    ones_ref, row_ref,
):
    ones = ones_ref[...]
    start = jnp.concatenate([before_ref[0], pltpu.roll(before_ref[1], UNIT, 1)], 0)
    wkv = out_ref[...] + wide_product(split2(query_ref[...]), split2(start))
    center = wkv - head_sum(wkv, ones) * (1.0 / UNIT)
    spread = head_sum(center * center, ones) * (1.0 / UNIT)
    normed = center * lax.rsqrt(spread + GROUP_EPS) * gain_ref[...] + shift_ref[...]
    mixed = (normed + bonus_ref[...]) * switch_ref[...].astype(F32) * live_ref[...]
    row_ref[...] = mixed.astype(BF16)


def finish(live, out, query, bonus, before, switch, gain, shift):
    tokens, width = out.shape
    places = np.arange(PAIR)
    ones = jnp.asarray(places[:, None] // UNIT == places[None, :] // UNIT, BF16)
    token_block = pl.BlockSpec((tokens, PAIR), lambda i: (0, i))
    row_block = pl.BlockSpec((1, PAIR), lambda i: (0, i))
    return pl.pallas_call(
        finish_kernel,
        grid=(width // PAIR,),
        in_specs=[pl.BlockSpec((tokens, 1), lambda i: (0, 0))]
        + [token_block] * 3
        + [pl.BlockSpec((2, UNIT, PAIR), lambda i: (i, 0, 0)), token_block]
        + [row_block] * 2
        + [pl.BlockSpec(ones.shape, lambda i: (0, 0))],
        out_specs=token_block,
        out_shape=jax.ShapeDtypeStruct((tokens, width), BF16),
        compiler_params=pltpu.CompilerParams(vmem_limit_bytes=24 * 1024 * 1024),
    )(live, out, query, bonus, before, switch, gain, shift, ones)


def per_device(
    sequence_sizes, acceptor, fading_scores, address_source, payload_source,
    learning_speed_scores, exit_switch, address_removal_factor, address_learning_factor,
    present_extra_factor, cluster_scale_term, cluster_shift_term, final_projection,
):
    tokens = acceptor.shape[1]
    weights = lax.all_gather(final_projection, ("req", "seq"), axis=0, tiled=True)
    position = lax.axis_index("seq") * tokens + jnp.arange(tokens, dtype=jnp.int32)
    live = (position < sequence_sizes[0]).astype(F32)[:, None]
    out, query, bonus, maps = local_pass(
        live, acceptor[0], fading_scores[0], address_source[0], payload_source[0],
        learning_speed_scores[0], address_removal_factor[None], address_learning_factor[None],
        present_extra_factor[None],
    )
    before = state_before(maps, "seq")
    mixed = finish(
        live, out, query, bonus, before, exit_switch[0], cluster_scale_term[None],
        cluster_shift_term[None],
    )
    projected = jnp.dot(mixed, weights, preferred_element_type=F32)
    return projected.astype(BF16)[None]


def solution(mesh):
    tokens = P("req", "seq", None)
    placed = (P("req"),) + (tokens,) * 6 + (P(),) * 5 + (P(("req", "seq"), None),)
    return jax.shard_map(
        per_device, mesh=mesh, in_specs=placed, out_specs=tokens, check_vma=False
    )
```

time: 1060 us -> 281 us (0.27); the launches traced: 1040 us -> 280 us
  other arithmetic: 373 us -> 0.02 us
  local copies, waits for them, and re-layouts: 226 us -> 10.8 us
  waiting for transfers between devices: 213 us -> 0.73 us
  matrix products: 203 us -> 11.5 us
  Pallas kernels: 0 us -> 181 us
  blocking collectives: 0 us -> 61.9 us
  loops' own time: 12.3 us -> 0 us
    another operation x12 -> x0, other arithmetic: 280 us -> none  [the longest x8 275 us: block_pass(): jax.scipy.linalg.solve_triangular(system, source, lower=True, unit_diagon...]
    pallas_call x0 -> x3, Pallas kernels: none -> 181 us  [the longest x1 169 us: local_pass(): pl.pallas_call(local_kernel, grid=(width // PAIR,), in_specs=[fixed((toke...]
    dot_general x54 -> x1, matrix products: 192 us -> 11.5 us  [per_device(): projected = jnp.dot(mixed, weights, preferred_element_type=F32)]
    all_gather x2 -> x0, waiting for transfers between devices: 149 us -> none  [prefix(): everything = jax.tree.map(lambda part: lax.all_gather(part, axis), array)]
    all_gather x1, waiting for transfers between devices: 63.5 us -> 0.02 us  [per_device(): lax.all_gather(final_projection, ('req', 'seq'), axis=0, tiled=True)]
    all_to_all x0 -> x2, blocking collectives: none -> 61.9 us  [the longest x1 32.8 us: state_before(): mine = lax.all_to_all(maps, axis, 0, 0, tiled=True)]
    dot_general x16 -> x0, local copies, waits for them, and re-layouts: 51.5 us -> none  [masked_pairs(): paired = jnp.einsum('thk,shk->hts', left_side, right_side, precision=EXACT)]
    select_n x8 -> x0, other arithmetic: 47.3 us -> none  [masked_pairs(): return jnp.where(keep_mask, paired, 0.0)]
  transfers between devices with their start and end apart: 3 -> 1, of which waited for: 3 -> 0; matrix products, arithmetic and copies ran while one was open for 7% -> 0% of each run, Pallas kernels for 0% -> 65%
where the time goes in v1:
time: 281 us; the launch traced here: 280 us
  Pallas kernels  181 us (64%)
  blocking collectives  61.9 us (22%)
  between operations  14.1 us (5%)
  matrix products  11.5 us (4%)
  local copies, waits for them, and re-layouts  10.8 us (4%)
    pallas_call x1, Pallas kernels, local_pass(): pl.pallas_call(local_kernel, grid=(width // PAIR,), in_specs=[fixed((toke...  169 us
    all_to_all x1, blocking collectives, state_before(): mine = lax.all_to_all(maps, axis, 0, 0, tiled=True)  32.8 us
    all_to_all x1, blocking collectives, state_before(): return lax.all_to_all(before, axis, 0, 0, tiled=True)  29 us
    dot_general x1, matrix products, per_device(): projected = jnp.dot(mixed, weights, preferred_element_type=F32)  11.5 us
    pallas_call x1, Pallas kernels, finish(): pl.pallas_call(finish_kernel, grid=(width // PAIR,), in_specs=[pl.BlockSp...  11.3 us
    unnamed x28, local copies, waits for them, and re-layouts  10.8 us
  transfers between devices with their start and end apart: 1, of which 0 were waited for; matrix products, arithmetic and copies ran while one was open for 0% of the time, Pallas kernels for 65%

profile of v1, /device:TPU:0, one launch (start us, length us, event | category | flops | bytes accessed | tf_op | source)
XLA Modules:
  0.0 280.4 jit_solution(900780667325644987)
XLA Ops:
  6.5 0.7 all-gather.2.cloned.1.call-update
  7.9 0.0 copy-start.1
  7.9 0.7 copy-done.1
  8.7 1.2 copy-done.4
  9.9 1.2 copy-done.5
  11.1 1.2 copy-done.6
  12.4 1.2 copy-done.7
  13.6 1.2 copy-done.8
  14.8 0.7 copy-done.9
  15.5 0.7 copy-done.10
  16.2 0.7 copy-done.11
  16.9 0.9 copy-done.12
  17.9 0.9 copy-done.13
  18.8 168.8 %shard_map.163 = (f32[256,2048]{1,0:T(8,128)S(1)}, f32[256,2048]{1,0:T(8,128)S(1)}, f32[256,2048]{1,0:T(8,128)S(1)}, f32[32,64,128]{2,1,0:T(8,128)S(1)}) custom-call(f32[256,1]{1,0:T(8,128)S(1)} %fusion.1.live_ref, bf16[256,2048]{1,0:T(8,128)(2,1)S(1)} %bitcast.20, bf16[256,2048]{1,0:T(8,128)(2,1)S(1)} %bitcast.21, bf16[256,2048]{1,0:T(8,128)(2,1)S(1)} %bitcast.22, ...), custom_call_target="tpu_custom_call" | custom-call | flops 60000002048 | bytes 12582912 | tf_op jit(solution)/shard_map/pallas_call | solution.py:179
  187.6 0.0 copy-start
  187.6 0.0 copy-start.2
  187.6 0.0 copy-start.3
  187.6 32.8 %all_to_all.10.map_ref = f32[32,64,128]{2,1,0:T(8,128)S(1)} all-to-all(f32[32,64,128]{2,1,0:T(8,128)S(1)} %get-tuple-element.12), channel_id=1, replica_groups=mesh['req'=4,'seq'=8] {'seq'}, dimensions={0} | all-to-all | bytes 2097152 | tf_op jit(solution)/shard_map/all_to_all | solution.py:217
  220.4 1.3 shard_map.164
  221.7 29.0 %all_to_all.11.before_ref = f32[32,64,128]{2,1,0:T(8,128)S(1)} all-to-all(f32[32,64,128]{2,1,0:T(8,128)S(1)} %shard_map.164), channel_id=1, replica_groups=mesh['req'=4,'seq'=8] {'seq'}, dimensions={0} | all-to-all | bytes 2097152 | tf_op jit(solution)/shard_map/all_to_all | solution.py:223
  250.7 0.0 copy-done.2
  250.7 11.3 %shard_map.165 = bf16[256,2048]{1,0:T(8,128)(2,1)S(1)} custom-call(f32[256,1]{1,0:T(8,128)S(1)} %fusion.1.live_ref, f32[256,2048]{1,0:T(8,128)S(1)} %get-tuple-element.9.out_ref, f32[256,2048]{1,0:T(8,128)S(1)} %get-tuple-element.10.query_ref, f32[256,2048]{1,0:T(8,128)S(1)} %get-tuple-element.11.bonus_ref, f32[32,64,128]{2,1,0:T(8,128)S(1)} %all_to_all.11.before_ref, ...), custom_call_target="tpu_custom_call" | custom-call | tf_op jit(solution)/shard_map/pallas_call | solution.py:246
  262.0 0.0 all-gather.2.cloned.1.call-done
  262.1 11.5 %fusion = bf16[1,256,4096]{2,1,0:T(8,128)(2,1)} fusion(bf16[256,2048]{1,0:T(8,128)(2,1)S(1)} %shard_map.165, bf16[2048,4096]{1,0:T(8,128)(2,1)} %all-gather.2.cloned.1.call-done), kind=kOutput, calls=%fused_computation.1 | convolution fusion | flops 4296015872 | bytes 19922944 | tf_op jit(solution)/shard_map/dot_general | solution.py:279
  (14 shorter events, 0.0 us)
Async XLA Ops:
  6.5 255.5 %all-gather.2.cloned.1.call-start = ((), (), s32[]{:S(2)}) async-start(), calls=%async_computation.2 | async-start | bytes 17301504 | tf_op jit(solution)/shard_map/all_gather | solution.py:266
  7.9 0.8 copy-start.1
  8.7 1.2 copy-start.4
  9.9 1.2 copy-start.5
  11.1 1.2 copy-start.6
  12.4 1.2 copy-start.7
  13.6 1.2 copy-start.8
  14.8 0.7 copy-start.9
  15.5 0.7 copy-start.10
  16.2 0.7 copy-start.11
  16.9 0.9 copy-start.12
  17.9 0.9 copy-start.13
  187.6 63.2 %copy-start = (bf16[1,256,2048]{2,1,0:T(8,128)(2,1)S(1)}, bf16[1,256,2048]{2,1,0:T(8,128)(2,1)}, u32[]{:S(2)}) copy-start(bf16[1,256,2048]{2,1,0:T(8,128)(2,1)} %param.23) | copy-start | bytes 3145732
  187.6 63.2 %copy-start.2 = (f32[2048]{0:T(1024)S(1)}, f32[2048]{0:T(1024)}, u32[]{:S(2)}) copy-start(f32[2048]{0:T(1024)} %param.27) | copy-start | bytes 24580
  187.6 63.2 %copy-start.3 = (f32[2048]{0:T(1024)S(1)}, f32[2048]{0:T(1024)}, u32[]{:S(2)}) copy-start(f32[2048]{0:T(1024)} %param.28) | copy-start | bytes 24580
Sparse Core Ops, SparseCore 0:
  10.4 119.0 all-gather.1

commit v2 on v1

v2 whole, which is shorter than its diff:
```python
import functools
import math

import jax
import jax.numpy as jnp
import numpy as np
from jax import lax
from jax.experimental import pallas as pl
from jax.experimental.pallas import tpu as pltpu
from jax.sharding import PartitionSpec as P

LOCAL_UNITS = 32
DECAY_SCALE = 0.606531
UNIT_EPS = 1e-06
GROUP_EPS = 0.00064
F32, BF16 = jnp.float32, jnp.bfloat16
UNIT = 64
PAIR = 128
GROUP = 2
FINISH_GROUP = 4


def split2(x):
    hi = x.astype(BF16)
    return hi, (x - hi.astype(F32)).astype(BF16)


def mm(a, b):
    return jnp.dot(a, b, preferred_element_type=F32)


def mm_t(a, b):
    return lax.dot_general(a, b, (((1,), (1,)), ((), ())), preferred_element_type=F32)


def square_product(a, b):
    (ah, al), (bh, bl) = a, b
    left = jnp.concatenate([ah, al], 1)
    row = jnp.concatenate([bh, bl], 1)
    both = mm(left, jnp.concatenate([row, row], 0))
    return both[:, :PAIR] + both[:, PAIR:]


def wide_product(a, b):
    (ah, al), (bh, bl) = a, b
    both = mm(ah, jnp.concatenate([bh, bl], 1))
    return both[:, :PAIR] + both[:, PAIR:] + mm(al, bh)


def head_sum(x, ones):
    hi, lo = split2(x)
    return mm(hi, ones) + mm(lo, ones)


def sigmoid(x):
    return 1.0 / (1.0 + jnp.exp(-x))


def local_kernel(
    live_ref, acc_ref, fade_ref, key_ref, val_ref, rate_ref, rem_ref, learn_ref, extra_ref,
    tri_ref, ones_ref, level_ref, out_ref, query_ref, bonus_ref, state_ref,
):
    tokens = acc_ref.shape[0]
    half = tokens // 2
    ones = ones_ref[...]
    tri = tri_ref[...]
    live = live_ref[...]
    lane = lax.broadcasted_iota(jnp.int32, (1, PAIR), 1)
    low = lane < UNIT
    rows = lax.broadcasted_iota(jnp.int32, (tokens, tokens), 0)
    columns = lax.broadcasted_iota(jnp.int32, (tokens, tokens), 1)
    strict, upto = rows > columns, rows >= columns
    eye = (rows[:half, :half] == columns[:half, :half]).astype(F32)
    krow = lax.broadcasted_iota(jnp.int32, (UNIT, PAIR), 0)
    klane = lax.broadcasted_iota(jnp.int32, (UNIT, PAIR), 1)
    levels = level_ref.shape[0]
    pairs_here = acc_ref.shape[1] // PAIR
    heads = []
    for p in range(pairs_here):
        span = slice(p * PAIR, (p + 1) * PAIR)
        rate = sigmoid(rate_ref[:, span].astype(F32))
        keys = key_ref[:, span].astype(F32)
        unit = keys * rem_ref[:, span]
        unit = unit * lax.rsqrt(head_sum(unit * unit, ones) + UNIT_EPS)
        key_mod = keys * (1.0 + (rate - 1.0) * learn_ref[:, span]) * live
        log_decay = -DECAY_SCALE * sigmoid(fade_ref[:, span].astype(F32)) * live
        values = val_ref[:, span] * live.astype(BF16)
        acc = acc_ref[:, span].astype(F32)
        bonus_ref[:, span] = (
            head_sum(acc * key_mod * extra_ref[:, span], ones) * values.astype(F32)
        )
        push = unit * (rate * live)
        first, rest = split2(log_decay)
        third = (log_decay - first.astype(F32) - rest.astype(F32)).astype(BF16)
        cumul = mm(tri, first) + (mm(tri, rest) + mm(tri, third))
        middle = cumul[half - 1 : half]
        last = cumul[tokens - 1 : tokens]
        up = jnp.exp(cumul - middle)
        down = jnp.exp(middle - cumul)
        to_middle = jnp.exp(middle)
        tail = jnp.exp(last - cumul)
        read_c = acc * up
        pull_c = -unit * jnp.exp(cumul - log_decay - middle)
        push_c = split2(push * down)
        key_c = split2(key_mod * down)
        push_tail = (push * tail).T
        key_tail = (key_mod * tail).T
        whole_decay = jnp.exp(last)
        right = jnp.concatenate([push_c[0], key_c[0]], 0)
        right_low = jnp.concatenate([push_c[1], key_c[1]], 0)
        right_twice = jnp.concatenate([right, right], 1)
        pulled_swap = pltpu.roll(pull_c * to_middle, UNIT, 1)
        read_swap = pltpu.roll(read_c * to_middle, UNIT, 1)
        decay_swap = pltpu.roll(whole_decay * jnp.ones((8, PAIR), F32), UNIT, 1)[:1]
        for h in range(2):
            mine = (lane // UNIT) == h
            ph, plow = split2(jnp.where(mine, pull_c, 0.0))
            rh, rlow = split2(jnp.where(mine, read_c, 0.0))
            left = jnp.concatenate(
                [jnp.concatenate([ph, plow], 1), jnp.concatenate([rh, rlow], 1)], 0
            )
            paired = mm_t(left, right_twice) + mm_t(jnp.concatenate([ph, rh], 0), right_low)
            a_pp = jnp.where(strict, paired[:tokens, :tokens], 0.0)
            a_pk = split2(jnp.where(strict, paired[:tokens, tokens:], 0.0))
            a_rp = split2(jnp.where(upto, paired[tokens:, :tokens], 0.0))
            a_rk = split2(jnp.where(upto, paired[tokens:, tokens:], 0.0))
            own = slice(h * UNIT, (h + 1) * UNIT)
            kt = split2(key_tail[own])
            source = jnp.where(mine, mm(a_pk[0], values) + mm(a_pk[1], values), pulled_swap)
            plain = jnp.where(mine, mm(a_rk[0], values) + mm(a_rk[1], values), read_swap)
            identity = jnp.where(klane == krow + (1 - h) * UNIT, decay_swap, 0.0)
            state = jnp.where(mine, mm(kt[0], values) + mm(kt[1], values), identity)
            heads.append((a_pp, a_rp, source, plain, state, split2(push_tail[own])))
    systems = [split2(head[0]) for head in heads]
    blocks, inverses = [], []
    for (a_pp, *_), (high, small) in zip(heads, systems):
        for b in range(2):
            cut = slice(b * half, (b + 1) * half)
            blocks.append((high[cut, cut], small[cut, cut]))
            inverses.append(eye + a_pp[cut, cut] * level_ref[0].astype(F32))
    for level in range(1, levels):
        mask = level_ref[level]
        now = [split2(inverse) for inverse in inverses]
        steps = [
            square_product((high * mask, small * mask), n)
            for (high, small), n in zip(blocks, now)
        ]
        steps = [split2(step) for step in steps]
        inverses = [
            inverse + square_product(n, step) for inverse, n, step in zip(inverses, now, steps)
        ]
    inverses = [split2(inverse) for inverse in inverses]
    count = len(heads)
    tops = [
        split2(square_product(inverses[2 * i], split2(heads[i][2][:half]))) for i in range(count)
    ]
    below = [
        heads[i][2][half:]
        + square_product((systems[i][0][half:, :half], systems[i][1][half:, :half]), tops[i])
        for i in range(count)
    ]
    bottoms = [
        split2(square_product(inverses[2 * i + 1], split2(below[i]))) for i in range(count)
    ]
    outs = []
    for i in range(count):
        removed = (
            jnp.concatenate([tops[i][0], bottoms[i][0]], 0),
            jnp.concatenate([tops[i][1], bottoms[i][1]], 0),
        )
        _, a_rp, _, plain, state, push_tail = heads[i]
        outs.append(wide_product(a_rp, removed) + plain)
        state = wide_product(push_tail, removed) + state
        if i % 2:
            state = pltpu.roll(state, UNIT, 1)
        state_ref[i] = jnp.where(klane == krow + UNIT, state - 1.0, state).astype(BF16)
    for p in range(pairs_here):
        span = slice(p * PAIR, (p + 1) * PAIR)
        even, odd = outs[2 * p], outs[2 * p + 1]
        out_ref[:, span] = jnp.where(low, even, odd)
        query_ref[:, span] = pltpu.roll(jnp.where(low, odd, even), UNIT, 1)


def local_pass(live, acceptor, fading, keys, values, rates, removal, learning, extra):
    tokens, width = acceptor.shape
    half = tokens // 2
    tri = jnp.asarray(np.tril(np.ones((tokens, tokens), np.float32)), BF16)
    places = np.arange(PAIR)
    ones = jnp.asarray(places[:, None] // UNIT == places[None, :] // UNIT, BF16)
    spots = np.arange(half)
    apart = spots[:, None] ^ spots[None, :]
    levels = jnp.asarray(
        np.stack([(apart >> n) == 1 for n in range(int(math.log2(half)))]), BF16
    )
    token_block = pl.BlockSpec((tokens, GROUP * PAIR), lambda i: (0, i))
    row_block = pl.BlockSpec((1, GROUP * PAIR), lambda i: (0, i))

    def fixed(shape):
        return pl.BlockSpec(shape, lambda i: (0,) * len(shape))

    return pl.pallas_call(
        local_kernel,
        grid=(width // (GROUP * PAIR),),
        in_specs=[fixed((tokens, 1))]
        + [token_block] * 5
        + [row_block] * 3
        + [fixed(tri.shape), fixed(ones.shape), fixed(levels.shape)],
        out_specs=[token_block] * 3 + [pl.BlockSpec((2 * GROUP, UNIT, PAIR), lambda i: (i, 0, 0))],
        out_shape=[jax.ShapeDtypeStruct((tokens, width), F32)] * 3
        + [jax.ShapeDtypeStruct((width // UNIT, UNIT, PAIR), BF16)],
        compiler_params=pltpu.CompilerParams(vmem_limit_bytes=56 * 1024 * 1024),
        cost_estimate=pl.CostEstimate(
            flops=60 * 10**9, bytes_accessed=12 * 2**20, transcendentals=3 * 10**6
        ),
    )(live, acceptor, fading, keys, values, rates, removal, learning, extra, tri, ones, levels)


def prefix_kernel(blocks, heads, map_ref, before_ref):
    low = lax.broadcasted_iota(jnp.int32, (1, PAIR), 1) < UNIT
    for h in range(heads):
        before_ref[h] = jnp.zeros((UNIT, PAIR), BF16)
    states = [jnp.where(low, map_ref[h].astype(F32), 0.0) for h in range(heads)]
    for n in range(1, blocks):
        for h in range(heads):
            high, small = split2(states[h])
            before_ref[n * heads + h] = jnp.where(
                low, high.astype(F32), pltpu.roll(small.astype(F32), UNIT, 1)
            ).astype(BF16)
            if n + 1 < blocks:
                step = map_ref[n * heads + h].astype(F32)
                transit = pltpu.roll(step, UNIT, 1)[:, :UNIT].astype(BF16)
                states[h] = (
                    states[h]
                    + jnp.where(low, step, 0.0)
                    + (mm(transit, high) + mm(transit, small))
                )


def state_before(maps, axis):
    blocks = lax.axis_size(axis)
    heads = maps.shape[0] // blocks
    mine = lax.all_to_all(maps, axis, 0, 0, tiled=True)
    before = pl.pallas_call(
        functools.partial(prefix_kernel, blocks, heads),
        out_shape=jax.ShapeDtypeStruct(mine.shape, BF16),
        compiler_params=pltpu.CompilerParams(vmem_limit_bytes=24 * 1024 * 1024),
    )(mine)
    return lax.all_to_all(before, axis, 0, 0, tiled=True)


def finish_kernel(
    live_ref, out_ref, query_ref, bonus_ref, before_ref, switch_ref, gain_ref, shift_ref,
    ones_ref, row_ref,
):
    ones = ones_ref[...]
    low = lax.broadcasted_iota(jnp.int32, (1, PAIR), 1) < UNIT
    for p in range(out_ref.shape[1] // PAIR):
        span = slice(p * PAIR, (p + 1) * PAIR)
        even, odd = before_ref[2 * p].astype(F32), before_ref[2 * p + 1].astype(F32)
        even_swap, odd_swap = pltpu.roll(even, UNIT, 1), pltpu.roll(odd, UNIT, 1)
        high = jnp.concatenate([jnp.where(low, even, 0.0), jnp.where(low, 0.0, odd_swap)], 0)
        small = jnp.concatenate([jnp.where(low, even_swap, 0.0), jnp.where(low, 0.0, odd)], 0)
        wkv = out_ref[:, span] + wide_product(
            split2(query_ref[:, span]), (high.astype(BF16), small.astype(BF16))
        )
        center = wkv - head_sum(wkv, ones) * (1.0 / UNIT)
        spread = head_sum(center * center, ones) * (1.0 / UNIT)
        normed = center * lax.rsqrt(spread + GROUP_EPS) * gain_ref[:, span] + shift_ref[:, span]
        mixed = (normed + bonus_ref[:, span]) * switch_ref[:, span].astype(F32) * live_ref[...]
        row_ref[:, span] = mixed.astype(BF16)


def finish(live, out, query, bonus, before, switch, gain, shift):
    tokens, width = out.shape
    places = np.arange(PAIR)
    ones = jnp.asarray(places[:, None] // UNIT == places[None, :] // UNIT, BF16)
    token_block = pl.BlockSpec((tokens, FINISH_GROUP * PAIR), lambda i: (0, i))
    row_block = pl.BlockSpec((1, FINISH_GROUP * PAIR), lambda i: (0, i))
    return pl.pallas_call(
        finish_kernel,
        grid=(width // (FINISH_GROUP * PAIR),),
        in_specs=[pl.BlockSpec((tokens, 1), lambda i: (0, 0))]
        + [token_block] * 3
        + [pl.BlockSpec((2 * FINISH_GROUP, UNIT, PAIR), lambda i: (i, 0, 0)), token_block]
        + [row_block] * 2
        + [pl.BlockSpec(ones.shape, lambda i: (0, 0))],
        out_specs=token_block,
        out_shape=jax.ShapeDtypeStruct((tokens, width), BF16),
        compiler_params=pltpu.CompilerParams(vmem_limit_bytes=24 * 1024 * 1024),
    )(live, out, query, bonus, before, switch, gain, shift, ones)


def per_device(
    sequence_sizes, acceptor, fading_scores, address_source, payload_source,
    learning_speed_scores, exit_switch, address_removal_factor, address_learning_factor,
    present_extra_factor, cluster_scale_term, cluster_shift_term, final_projection,
):
    tokens = acceptor.shape[1]
    weights = lax.all_gather(final_projection, ("req", "seq"), axis=0, tiled=True)
    position = lax.axis_index("seq") * tokens + jnp.arange(tokens, dtype=jnp.int32)
    live = (position < sequence_sizes[0]).astype(F32)[:, None]
    out, query, bonus, maps = local_pass(
        live, acceptor[0], fading_scores[0], address_source[0], payload_source[0],
        learning_speed_scores[0], address_removal_factor[None], address_learning_factor[None],
        present_extra_factor[None],
    )
    before = state_before(maps, "seq")
    mixed = finish(
        live, out, query, bonus, before, exit_switch[0], cluster_scale_term[None],
        cluster_shift_term[None],
    )
    projected = jnp.dot(mixed, weights, preferred_element_type=F32)
    return projected.astype(BF16)[None]


def solution(mesh):
    tokens = P("req", "seq", None)
    placed = (P("req"),) + (tokens,) * 6 + (P(),) * 5 + (P(("req", "seq"), None),)
    return jax.shard_map(
        per_device, mesh=mesh, in_specs=placed, out_specs=tokens, check_vma=False
    )
```

time: 281 us -> 160 us (0.57)
  Pallas kernels: 181 us -> 59.7 us
  local copies, waits for them, and re-layouts: 10.8 us -> 3.24 us
  waiting for transfers between devices: 0.73 us -> 6.26 us
    pallas_call x2, Pallas kernels: 180 us -> 58.6 us  [the longest x1 51 us: local_pass(): pl.pallas_call(local_kernel, grid=(width // (GROUP * PAIR),), in_specs=[f...]
    unnamed x28 -> x16, local copies, waits for them, and re-layouts: 10.8 us -> 3.24 us
    all_gather x1, waiting for transfers between devices: 0.02 us -> 5.55 us  [per_device(): lax.all_gather(final_projection, ('req', 'seq'), axis=0, tiled=True)]
    all_to_all x1, blocking collectives: 29 us -> 33.8 us  [state_before(): return lax.all_to_all(before, axis, 0, 0, tiled=True)]
    all_to_all x1, blocking collectives: 32.8 us -> 30 us  [state_before(): mine = lax.all_to_all(maps, axis, 0, 0, tiled=True)]
  transfers between devices with their start and end apart: 1 -> 1, of which waited for: 0 -> 1; matrix products, arithmetic and copies ran while one was open for 0% -> 0% of each run, Pallas kernels for 65% -> 37%
where the time goes in v2:
time: 160 us; the launch traced here: 159 us
  blocking collectives  63.8 us (40%)
  Pallas kernels  59.7 us (37%)
  between operations  14.1 us (9%)
  matrix products  11.4 us (7%)
  waiting for transfers between devices  6.26 us (4%)
  local copies, waits for them, and re-layouts  3.24 us (2%)
    pallas_call x1, Pallas kernels, local_pass(): pl.pallas_call(local_kernel, grid=(width // (GROUP * PAIR),), in_specs=[f...  51 us
    all_to_all x1, blocking collectives, state_before(): return lax.all_to_all(before, axis, 0, 0, tiled=True)  33.8 us
    all_to_all x1, blocking collectives, state_before(): mine = lax.all_to_all(maps, axis, 0, 0, tiled=True)  30 us
    dot_general x1, matrix products, per_device(): projected = jnp.dot(mixed, weights, preferred_element_type=F32)  11.4 us
    pallas_call x1, Pallas kernels, finish(): pl.pallas_call(finish_kernel, grid=(width // (FINISH_GROUP * PAIR),), in_...  7.65 us
    all_gather x1, waiting for transfers between devices, per_device(): lax.all_gather(final_projection, ('req', 'seq'), axis=0, tiled=True)  5.55 us
    unnamed x16, local copies, waits for them, and re-layouts  3.24 us
  transfers between devices with their start and end apart: 1, of which 1 were waited for; matrix products, arithmetic and copies ran while one was open for 0% of the time, Pallas kernels for 37%

profile of v2, /device:TPU:0, one launch (start us, length us, event | category | flops | bytes accessed | tf_op | source)
XLA Modules:
  0.0 159.2 jit_solution(4321221209383994578)
XLA Ops:
  6.5 0.0 all-gather.2.cloned.1.call-start
  6.5 0.7 all-gather.2.cloned.1.call-update
  7.9 0.7 fusion.1.live_ref
  8.6 0.0 copy-start.3
  8.6 0.0 copy-start.4
  8.6 0.0 copy-start.5
  8.6 0.0 copy-start.7
  8.6 51.0 %shard_map.163 = (f32[256,2048]{1,0:T(8,128)}, f32[256,2048]{1,0:T(8,128)}, f32[256,2048]{1,0:T(8,128)}, bf16[32,64,128]{2,1,0:T(8,128)(2,1)}) custom-call(f32[256,1]{1,0:T(8,128)} %fusion.1.live_ref, bf16[256,2048]{1,0:T(8,128)(2,1)} %bitcast.20, bf16[256,2048]{1,0:T(8,128)(2,1)} %bitcast.21, bf16[256,2048]{1,0:T(8,128)(2,1)} %bitcast.22, ...), custom_call_target="tpu_custom_call" | custom-call | flops 60000002048 | bytes 12582912 | tf_op jit(solution)/shard_map/pallas_call | solution.py:201
  59.6 0.0 copy-start
  59.6 30.0 %all_to_all.10.map_ref = bf16[32,64,128]{2,1,0:T(8,128)(2,1)S(1)} all-to-all(bf16[32,64,128]{2,1,0:T(8,128)(2,1)} %get-tuple-element.12), channel_id=1, replica_groups=mesh['req'=4,'seq'=8] {'seq'}, dimensions={0} | all-to-all | bytes 1048576 | tf_op jit(solution)/shard_map/all_to_all | solution.py:242
  89.6 1.1 shard_map.164
  90.6 33.8 %all_to_all.11.before_ref = bf16[32,64,128]{2,1,0:T(8,128)(2,1)S(1)} all-to-all(bf16[32,64,128]{2,1,0:T(8,128)(2,1)S(1)} %shard_map.164), channel_id=1, replica_groups=mesh['req'=4,'seq'=8] {'seq'}, dimensions={0} | all-to-all | bytes 1048576 | tf_op jit(solution)/shard_map/all_to_all | solution.py:248
  124.5 0.0 copy-done.3
  124.5 0.0 copy-done.4
  124.5 0.0 copy-done.5
  124.5 0.0 copy-done.6
  124.5 0.0 copy-done.7
  124.5 0.0 copy-done
  124.5 0.0 copy-start.1
  124.5 1.6 copy-done.1
  126.1 1.6 %copy-done.2 = f32[256,2048]{1,0:T(8,128)S(1)} copy-done((f32[256,2048]{1,0:T(8,128)S(1)}, f32[256,2048]{1,0:T(8,128)}, u32[]{:S(2)}) %copy-start.2) | copy-done | bytes 2097176
  127.7 7.6 %shard_map.165 = bf16[256,2048]{1,0:T(8,128)(2,1)S(1)} custom-call(f32[256,1]{1,0:T(8,128)S(1)} %copy-done.4, f32[256,2048]{1,0:T(8,128)S(1)} %copy-done, f32[256,2048]{1,0:T(8,128)S(1)} %copy-done.1, f32[256,2048]{1,0:T(8,128)S(1)} %copy-done.2, bf16[32,64,128]{2,1,0:T(8,128)(2,1)S(1)} %all_to_all.11.before_ref, bf16[256,2048]{1,0:T(8,128)(2,1)S(1)} %bitcast.17, ...), custom_call_target="tpu_custom_call" | custom-call | tf_op jit(solution)/shard_map/pallas_call | solution.py:279
  135.4 5.5 %all-gather.2.cloned.1.call-done = bf16[2048,4096]{1,0:T(8,128)(2,1)} async-done(((bf16[64,4096]{1,0:T(8,128)(2,1)}), bf16[2048,4096]{1,0:T(8,128)(2,1)}) %all-gather.2.cloned.1.call-update) | async-done | bytes 16777232 | tf_op jit(solution)/shard_map/all_gather | solution.py:299
  140.9 11.4 %fusion = bf16[1,256,4096]{2,1,0:T(8,128)(2,1)} fusion(bf16[256,2048]{1,0:T(8,128)(2,1)S(1)} %shard_map.165, bf16[2048,4096]{1,0:T(8,128)(2,1)} %all-gather.2.cloned.1.call-done), kind=kOutput, calls=%fused_computation.1 | convolution fusion | flops 4296015872 | bytes 19922944 | tf_op jit(solution)/shard_map/dot_general | solution.py:312
  (2 shorter events, 0.0 us)
Async XLA Ops:
  6.5 134.4 %all-gather.2.cloned.1.call-start = ((), (), s32[]{:S(2)}) async-start(), calls=%async_computation.2 | async-start | bytes 17301504 | tf_op jit(solution)/shard_map/all_gather | solution.py:299
  8.6 115.9 %copy-start.3 = (bf16[1,256,2048]{2,1,0:T(8,128)(2,1)S(1)}, bf16[1,256,2048]{2,1,0:T(8,128)(2,1)}, u32[]{:S(2)}) copy-start(bf16[1,256,2048]{2,1,0:T(8,128)(2,1)} %param.23) | copy-start | bytes 3145732
  8.6 115.9 %copy-start.4 = (f32[256,1]{1,0:T(8,128)S(1)}, f32[256,1]{1,0:T(8,128)}, u32[]{:S(2)}) copy-start(f32[256,1]{1,0:T(8,128)} %fusion.1.live_ref) | copy-start | bytes 3076
  8.6 115.9 %copy-start.5 = (bf16[128,128]{1,0:T(8,128)(2,1)S(1)}, bf16[128,128]{1,0:T(8,128)(2,1)}, u32[]{:S(2)}) copy-start(bf16[128,128]{1,0:T(8,128)(2,1)} %constant.13.clone.ones_ref) | copy-start | bytes 98308
  8.6 115.9 %copy-start.6 = (f32[2048]{0:T(1024)S(1)}, f32[2048]{0:T(1024)}, u32[]{:S(2)}) copy-start(f32[2048]{0:T(1024)} %param.27) | copy-start | bytes 24580
  8.6 115.9 %copy-start.7 = (f32[2048]{0:T(1024)S(1)}, f32[2048]{0:T(1024)}, u32[]{:S(2)}) copy-start(f32[2048]{0:T(1024)} %param.28) | copy-start | bytes 24580
  59.6 64.9 %copy-start = (f32[256,2048]{1,0:T(8,128)S(1)}, f32[256,2048]{1,0:T(8,128)}, u32[]{:S(2)}) copy-start(f32[256,2048]{1,0:T(8,128)} %get-tuple-element.9.out_ref) | copy-start | bytes 6291460
  124.5 1.6 copy-start.1
  126.1 1.6 %copy-start.2 = (f32[256,2048]{1,0:T(8,128)S(1)}, f32[256,2048]{1,0:T(8,128)}, u32[]{:S(2)}) copy-start(f32[256,2048]{1,0:T(8,128)} %get-tuple-element.11.bonus_ref) | copy-start | bytes 6291460
Sparse Core Ops, SparseCore 0:
  10.4 130.5 all-gather.1

commit v3 on v2

--- a/solution.py
+++ b/solution.py
@@ -296,7 +296,10 @@
     present_extra_factor, cluster_scale_term, cluster_shift_term, final_projection,
 ):
     tokens = acceptor.shape[1]
-    weights = lax.all_gather(final_projection, ("req", "seq"), axis=0, tiled=True)
+    weights = [
+        lax.all_gather(part, ("req", "seq"), axis=0, tiled=True)
+        for part in jnp.split(final_projection, 2, 1)
+    ]
     position = lax.axis_index("seq") * tokens + jnp.arange(tokens, dtype=jnp.int32)
     live = (position < sequence_sizes[0]).astype(F32)[:, None]
     out, query, bonus, maps = local_pass(
@@ -309,8 +312,8 @@
         live, out, query, bonus, before, exit_switch[0], cluster_scale_term[None],
         cluster_shift_term[None],
     )
-    projected = jnp.dot(mixed, weights, preferred_element_type=F32)
-    return projected.astype(BF16)[None]
+    projected = [jnp.dot(mixed, part, preferred_element_type=F32).astype(BF16) for part in weights]
+    return jnp.concatenate(projected, 1)[None]
 
 
 def solution(mesh):

time: 160 us -> 194 us (1.21)
  waiting for transfers between devices: 6.26 us -> 46.2 us
  blocking collectives: 63.8 us -> 54.8 us
    all_gather x1 -> x2, waiting for transfers between devices: 5.55 us -> 45.5 us  [per_device(): lax.all_gather(part, ('req', 'seq'), axis=0, tiled=True)]
    all_to_all x1, blocking collectives: 33.8 us -> 19.8 us  [state_before(): return lax.all_to_all(before, axis, 0, 0, tiled=True)]
    all_to_all x1, blocking collectives: 30 us -> 35 us  [state_before(): mine = lax.all_to_all(maps, axis, 0, 0, tiled=True)]
    dot_general x1 -> x2, matrix products: 11.4 us -> 11.4 us  [per_device(): jnp.dot(mixed, part, preferred_element_type=F32).astype(BF16)]
  transfers between devices with their start and end apart: 1 -> 2, of which waited for: 1 -> 1; matrix products, arithmetic and copies ran while one was open for 0% -> 3% of each run, Pallas kernels for 37% -> 31%
where the time goes in v3:
time: 194 us
  Pallas kernels  59.7 us (31%)
  blocking collectives  54.8 us (28%)
  waiting for transfers between devices  46.2 us (24%)
  between operations  14.2 us (7%)
  matrix products  11.4 us (6%)
  local copies, waits for them, and re-layouts  5.09 us (3%)
  other arithmetic  2.18 us (1%)
    pallas_call x1, Pallas kernels, local_pass(): pl.pallas_call(local_kernel, grid=(width // (GROUP * PAIR),), in_specs=[f...  51 us
    all_gather x2, waiting for transfers between devices, per_device(): lax.all_gather(part, ('req', 'seq'), axis=0, tiled=True)  45.5 us
    all_to_all x1, blocking collectives, state_before(): mine = lax.all_to_all(maps, axis, 0, 0, tiled=True)  35 us
    all_to_all x1, blocking collectives, state_before(): return lax.all_to_all(before, axis, 0, 0, tiled=True)  19.8 us
    dot_general x2, matrix products, per_device(): jnp.dot(mixed, part, preferred_element_type=F32).astype(BF16)  11.4 us
    pallas_call x1, Pallas kernels, finish(): pl.pallas_call(finish_kernel, grid=(width // (FINISH_GROUP * PAIR),), in_...  7.65 us
  transfers between devices with their start and end apart: 2, of which 1 were waited for; matrix products, arithmetic and copies ran while one was open for 3% of the time, Pallas kernels for 31%

profile of v3, /device:TPU:0, one launch (start us, length us, event | category | flops | bytes accessed | tf_op | source)
XLA Modules:
  0.0 193.5 jit_solution(11894989677745589435)
XLA Ops:
  6.5 0.0 all-gather.5.cloned.1.call-start
  6.5 1.9 fusion.1
  8.4 0.0 all-gather.5.cloned.1.call-update
  8.4 0.0 all-gather.3.cloned.1.call-start
  8.5 0.7 all-gather.3.cloned.1.call-update
  9.8 0.7 fusion.live_ref
  10.5 0.0 copy-start.7
  10.5 51.0 %shard_map.163 = (f32[256,2048]{1,0:T(8,128)}, f32[256,2048]{1,0:T(8,128)}, f32[256,2048]{1,0:T(8,128)}, bf16[32,64,128]{2,1,0:T(8,128)(2,1)}) custom-call(f32[256,1]{1,0:T(8,128)} %fusion.live_ref, bf16[256,2048]{1,0:T(8,128)(2,1)} %bitcast.22, bf16[256,2048]{1,0:T(8,128)(2,1)} %bitcast.23, bf16[256,2048]{1,0:T(8,128)(2,1)} %bitcast.24, ...), custom_call_target="tpu_custom_call" | custom-call | flops 60000002048 | bytes 12582912 | tf_op jit(solution)/shard_map/pallas_call | solution.py:201
  61.5 0.0 copy-start
  61.5 35.0 %all_to_all.10.map_ref = bf16[32,64,128]{2,1,0:T(8,128)(2,1)S(1)} all-to-all(bf16[32,64,128]{2,1,0:T(8,128)(2,1)} %get-tuple-element.12), channel_id=1, replica_groups=mesh['req'=4,'seq'=8] {'seq'}, dimensions={0} | all-to-all | bytes 1048576 | tf_op jit(solution)/shard_map/all_to_all | solution.py:242
  96.5 1.1 shard_map.164
  97.6 19.8 %all_to_all.11.before_ref = bf16[32,64,128]{2,1,0:T(8,128)(2,1)S(1)} all-to-all(bf16[32,64,128]{2,1,0:T(8,128)(2,1)S(1)} %shard_map.164), channel_id=1, replica_groups=mesh['req'=4,'seq'=8] {'seq'}, dimensions={0} | all-to-all | bytes 1048576 | tf_op jit(solution)/shard_map/all_to_all | solution.py:248
  117.4 0.0 copy-done.3
  117.4 0.0 copy-done.4
  117.4 0.0 copy-done.5
  117.4 0.0 copy-done.6
  117.4 1.6 copy-done.1
  119.0 1.6 copy-done.2
  120.6 7.7 %shard_map.165 = bf16[256,2048]{1,0:T(8,128)(2,1)S(1)} custom-call(f32[256,1]{1,0:T(8,128)S(1)} %copy-done.4, f32[256,2048]{1,0:T(8,128)S(1)} %copy-done, f32[256,2048]{1,0:T(8,128)S(1)} %copy-done.1, f32[256,2048]{1,0:T(8,128)S(1)} %copy-done.2, bf16[32,64,128]{2,1,0:T(8,128)(2,1)S(1)} %all_to_all.11.before_ref, bf16[256,2048]{1,0:T(8,128)(2,1)S(1)} %bitcast.19, ...), custom_call_target="tpu_custom_call" | custom-call | tf_op jit(solution)/shard_map/pallas_call | solution.py:279
  128.3 0.0 all-gather.5.cloned.1.call-done
  128.3 5.7 %convolution_convert_fusion = bf16[256,2048]{1,0:T(8,128)(2,1)S(1)} fusion(bf16[256,2048]{1,0:T(8,128)(2,1)S(1)} %shard_map.165, bf16[2048,2048]{1,0:T(8,128)(2,1)} %all-gather.5.cloned.1.call-done), kind=kOutput, calls=%fused_computation | convolution fusion | flops 2148007936 | bytes 10485760 | tf_op jit(solution)/shard_map/dot_general | solution.py:315
  134.0 45.5 %all-gather.3.cloned.1.call-done = bf16[2048,2048]{1,0:T(8,128)(2,1)} async-done(((bf16[64,2048]{1,0:T(8,128)(2,1)}), bf16[2048,2048]{1,0:T(8,128)(2,1)}) %all-gather.3.cloned.1.call-update) | async-done | bytes 8388624 | tf_op jit(solution)/shard_map/all_gather | solution.py:300
  179.5 5.7 %convolution_convert_fusion.1 = bf16[256,2048]{1,0:T(8,128)(2,1)S(1)} fusion(bf16[256,2048]{1,0:T(8,128)(2,1)S(1)} %shard_map.165, bf16[2048,2048]{1,0:T(8,128)(2,1)} %all-gather.3.cloned.1.call-done), kind=kOutput, calls=%fused_computation.1 | convolution fusion | flops 2148007936 | bytes 10485760 | tf_op jit(solution)/shard_map/dot_general | solution.py:315
  185.2 1.5 maximum_bitcast_fusion
  (8 shorter events, 0.0 us)
Async XLA Ops:
  6.5 121.7 %all-gather.5.cloned.1.call-start = ((), (), s32[]{:S(2)}) async-start(), calls=%async_computation.3 | async-start | bytes 8650752 | tf_op jit(solution)/shard_map/all_gather | solution.py:300
  8.4 171.0 %all-gather.3.cloned.1.call-start = ((), (), s32[]{:S(2)}) async-start(), calls=%async_computation.2 | async-start | bytes 8650752 | tf_op jit(solution)/shard_map/all_gather | solution.py:300
  10.5 106.8 %copy-start.3 = (bf16[1,256,2048]{2,1,0:T(8,128)(2,1)S(1)}, bf16[1,256,2048]{2,1,0:T(8,128)(2,1)}, u32[]{:S(2)}) copy-start(bf16[1,256,2048]{2,1,0:T(8,128)(2,1)} %param.23) | copy-start | bytes 3145732
  10.5 106.8 %copy-start.4 = (f32[256,1]{1,0:T(8,128)S(1)}, f32[256,1]{1,0:T(8,128)}, u32[]{:S(2)}) copy-start(f32[256,1]{1,0:T(8,128)} %fusion.live_ref) | copy-start | bytes 3076
  10.5 106.8 %copy-start.5 = (bf16[128,128]{1,0:T(8,128)(2,1)S(1)}, bf16[128,128]{1,0:T(8,128)(2,1)}, u32[]{:S(2)}) copy-start(bf16[128,128]{1,0:T(8,128)(2,1)} %constant.13.clone.ones_ref) | copy-start | bytes 98308
  10.5 106.8 %copy-start.6 = (f32[2048]{0:T(1024)S(1)}, f32[2048]{0:T(1024)}, u32[]{:S(2)}) copy-start(f32[2048]{0:T(1024)} %param.27) | copy-start | bytes 24580
  10.5 106.8 %copy-start.7 = (f32[2048]{0:T(1024)S(1)}, f32[2048]{0:T(1024)}, u32[]{:S(2)}) copy-start(f32[2048]{0:T(1024)} %param.28) | copy-start | bytes 24580
  61.5 55.9 %copy-start = (f32[256,2048]{1,0:T(8,128)S(1)}, f32[256,2048]{1,0:T(8,128)}, u32[]{:S(2)}) copy-start(f32[256,2048]{1,0:T(8,128)} %get-tuple-element.9.out_ref) | copy-start | bytes 6291460
  117.4 1.6 copy-start.1
  119.0 1.6 copy-start.2
Sparse Core Ops, SparseCore 0:
  10.3 89.1 all-gather.4
  102.5 76.8 all-gather.2
